TPU v7x, 512 devices: a whole 4x4x16 slice. The times are simulated.
512 devices in a mesh: grp: 4 (over y), comp: 16 (over z_hi, x, core), tp: 8 (over z_lo).
Axes of the slice: x: 4, y: 4, z: 16 (z_hi: 2, z_lo: 8; z = z_hi * 8 + z_lo), core: 2. Of those that a mesh axis runs over, the one named last changes fastest.
Arguments:
- queries: bfloat16 [16384, 8192], P(('grp', 'comp'), 'tp'), parts along dimension 0, may hold values from -18 to 18
- comp_keys: bfloat16 [16384, 1024], P(('grp', 'comp'), 'tp'), parts along dimension 0, may hold values from -6 to 6
- comp_values: bfloat16 [16384, 1024], P(('grp', 'comp'), 'tp'), parts along dimension 0, may hold values from -6 to 6
- prompt_keys: bfloat16 [6144, 1024], P(('grp', 'comp'), 'tp'), parts along dimension 0, may hold values from -16 to 16
- prompt_values: bfloat16 [6144, 1024], P(('grp', 'comp'), 'tp'), parts along dimension 0, may hold values from -6 to 6
- upstream: bfloat16 [16384, 8192], P(('grp', 'comp'), 'tp'), parts along dimension 0, may hold values from -48 to 48
- rewards: float32 [64], P(('grp', 'comp')), parts along dimension 0, may hold values from 0 to 3
- lengths: int32 [64], P(('grp', 'comp')), parts along dimension 0, may hold values from 128 to 256, as said below
Outputs:
- query_grad: bfloat16 [16384, 8192], P(('grp', 'comp'), 'tp'), parts along dimension 0
- comp_key_grad: bfloat16 [16384, 1024], P(('grp', 'comp'), 'tp'), parts along dimension 0
- comp_value_grad: bfloat16 [16384, 1024], P(('grp', 'comp'), 'tp'), parts along dimension 0
- prompt_key_grad: bfloat16 [6144, 1024], P(('grp', 'comp'), 'tp'), parts along dimension 0
- prompt_value_grad: bfloat16 [6144, 1024], P(('grp', 'comp'), 'tp'), parts along dimension 0
There are 4 independent parts, one for each index of `grp`. A program takes and returns all parts, laid end to end along the dimension named above; each array names one. Nothing has to cross between parts.
Inputs may be any that keep to these rules, and one draw needn't show every extreme that they name: lengths are multiples of 128; in every group one completion has all 256 slots valid.
All inputs are finite; a program needn't handle non-finite values.
Results may differ from a plain program's by a relative error of at most 0.0061.
Values may be sent and summed in bfloat16 or wider, within the bound.
A program may use at most 64 MiB of HBM per device.

v0:
```python
import jax
import jax.numpy as jnp
from jax import lax
from jax.sharding import PartitionSpec as P

D_HEAD = 128


NEG = -1e30


def split_heads(block, groups):
    rows = block.shape[0]
    return block.reshape(rows, groups, -1, D_HEAD).transpose(1, 2, 0, 3)


def split_kv(block, groups):
    rows = block.shape[0]
    return block.reshape(rows, groups, D_HEAD).transpose(1, 0, 2)


def join_kv(block):
    groups, rows, width = block.shape
    return block.transpose(1, 0, 2).reshape(rows, groups * width)


def head_terms(query_head, cot_head, keys, values, keep):
    scale = D_HEAD ** (-0.5)
    scores = jnp.dot(query_head, keys.T, preferred_element_type=jnp.float32) * scale
    scores = jnp.where(keep, scores, NEG)
    top = jnp.max(scores, axis=1, keepdims=True)
    lse = top + jnp.log(jnp.sum(jnp.exp(scores - top), axis=1, keepdims=True))
    probs = jnp.exp(scores - lse)
    probs_half = probs.astype(jnp.bfloat16)
    attended = jnp.dot(probs_half, values, preferred_element_type=jnp.float32).astype(jnp.bfloat16)
    attended = lax.optimization_barrier(attended)
    delta = jnp.sum(
        cot_head.astype(jnp.float32) * attended.astype(jnp.float32), axis=1, keepdims=True
    )
    dprobs = jnp.dot(cot_head, values.T, preferred_element_type=jnp.float32)
    dscores = (probs * (dprobs - delta)).astype(jnp.bfloat16)
    return (lse, delta, probs_half, dscores)


def attend(query, cot, comp_k, comp_v, prompt_k, prompt_v, first):
    scale = D_HEAD ** (-0.5)
    groups = comp_k.shape[1] // D_HEAD
    rows = query.shape[0]
    span = prompt_k.shape[0]
    keys = jnp.concatenate([prompt_k, comp_k], 0)
    values = jnp.concatenate([prompt_v, comp_v], 0)
    row_pos = lax.broadcasted_iota(jnp.int32, (rows, span + rows), 0)
    col_pos = lax.broadcasted_iota(jnp.int32, (rows, span + rows), 1)
    keep = (col_pos < span) | (col_pos - span <= row_pos)

    def one_group(operands):
        query_group, cot_group, key_group, value_group = operands

        def one_head(totals, pair):
            query_head, cot_head = pair
            lse, delta, probs_half, dscores = head_terms(
                query_head, cot_head, key_group, value_group, keep
            )
            dquery = jnp.dot(dscores, key_group, preferred_element_type=jnp.float32) * scale
            dkey = jnp.dot(dscores.T, query_head, preferred_element_type=jnp.float32) * scale
            dvalue = jnp.dot(probs_half.T, cot_head, preferred_element_type=jnp.float32)
            return ((totals[0] + dkey, totals[1] + dvalue), (dquery, lse, delta))

        empty = jnp.zeros((span + rows - first, D_HEAD), jnp.float32)
        (dkey, dvalue), (dquery, lse, delta) = lax.scan(
            one_head, (empty, empty), (query_group, cot_group)
        )
        return (dkey, dvalue, dquery, lse, delta)

    dkey, dvalue, dquery, lse, delta = lax.map(
        one_group,
        (
            split_heads(query, groups),
            split_heads(cot, groups),
            split_kv(keys, groups),
            split_kv(values, groups),
        ),
    )
    dquery = dquery.transpose(2, 0, 1, 3).reshape(rows, -1)
    return (dquery, join_kv(dkey), join_kv(dvalue), lse, delta)


def shards(queries, comp_keys, comp_values, prompt_keys, prompt_values, upstream, rewards, lengths):
    group_size = lax.axis_size("comp")
    reward_sum = lax.psum(jnp.sum(rewards), "comp")
    advantage = rewards[0] - reward_sum / group_size
    all_keys, all_values = (
        lax.all_gather(prompt_keys, "comp", axis=0, tiled=True),
        lax.all_gather(prompt_values, "comp", axis=0, tiled=True),
    )
    slots = queries.shape[0]
    span = all_keys.shape[0]
    width = prompt_keys.shape[1]
    positions = jnp.arange(slots, dtype=jnp.int32)
    cot = jnp.where((positions < lengths[0])[:, None], upstream, jnp.zeros_like(upstream))
    dquery, dkey, dvalue, lse, delta = attend(
        queries, cot, comp_keys, comp_values, all_keys, all_values, 0
    )
    terms = advantage * jnp.concatenate([dkey[:span], dvalue[:span]], axis=1)
    summed = lax.psum_scatter(terms, "comp", scatter_dimension=0, tiled=True)
    comp_dkey = dkey[span:]
    comp_dvalue = dvalue[span:]
    query_grad = (advantage * dquery).astype(jnp.bfloat16)
    comp_key_grad = (advantage * comp_dkey).astype(jnp.bfloat16)
    comp_value_grad = (advantage * comp_dvalue).astype(jnp.bfloat16)
    prompt_key_grad = summed[:, :width].astype(jnp.bfloat16)
    prompt_value_grad = summed[:, width:].astype(jnp.bfloat16)
    return (query_grad, comp_key_grad, comp_value_grad, prompt_key_grad, prompt_value_grad)


def solution(mesh):
    in_specs = (
        P(("grp", "comp"), "tp"),
        P(("grp", "comp"), "tp"),
        P(("grp", "comp"), "tp"),
        P(("grp", "comp"), "tp"),
        P(("grp", "comp"), "tp"),
        P(("grp", "comp"), "tp"),
        P(("grp", "comp")),
        P(("grp", "comp")),
    )
    out_specs = (
        P(("grp", "comp"), "tp"),
        P(("grp", "comp"), "tp"),
        P(("grp", "comp"), "tp"),
        P(("grp", "comp"), "tp"),
        P(("grp", "comp"), "tp"),
    )
    return jax.shard_map(shards, mesh=mesh, in_specs=in_specs, out_specs=out_specs, check_vma=False)
```

profile of v0, /device:TPU:1, one launch (start us, length us, event | category | flops | bytes accessed | tf_op | source)
XLA Modules:
  0.0 360.4 jit_solution(1169262763089158430)
XLA Ops:
  7.3 1.3 copy.15
  9.3 52.2 %all_gather.6 = bf16[1536,128]{1,0:T(8,128)(2,1)S(1)} all-gather(bf16[96,128]{1,0:T(8,128)(2,1)} %param.13), channel_id=1, replica_groups=mesh['grp'=4,'comp'=16,'tp'=8] {'comp'}, dimensions={0}, use_global_device_ids=true | all-gather | bytes 417792 | tf_op jit(solution)/shard_map/all_gather | solution.py:93
  61.5 35.0 %all_gather.7 = bf16[1536,128]{1,0:T(8,128)(2,1)S(1)} all-gather(bf16[96,128]{1,0:T(8,128)(2,1)} %param.14), channel_id=1, replica_groups=mesh['grp'=4,'comp'=16,'tp'=8] {'comp'}, dimensions={0}, use_global_device_ids=true | all-gather | bytes 417792 | tf_op jit(solution)/shard_map/all_gather | solution.py:94
  99.2 79.2 %while.26 = (s32[]{:T(128)}, f32[1792,128]{1,0:T(8,128)S(1)}, f32[1792,128]{1,0:T(8,128)}, f32[8,256,128]{2,1,0:T(8,128)}, bf16[8,256,128]{1,2,0:T(8,128)(2,1)},...) while((s32[]{:T(128)}, f32[1792,128]{1,0:T(8,128)S(1)}, ...), condition=%wide.region_5.6_spmd.clone, body=%wide.region_1.5_spmd.clone.sunk | while | flops 712867328 | bytes 20141472 | solution.py:70
  99.2 1.8 fusion.55
  102.3 1.5 convolution_add_fusion.2
  106.4 1.6 fusion.57
  108.1 1.8 fusion.55
  111.1 2.7 convolution_add_fusion.2
  116.5 1.6 fusion.57
  118.1 1.8 fusion.55
  121.1 2.7 convolution_add_fusion.2
  126.5 1.6 fusion.57
  128.1 1.8 fusion.55
  131.2 2.7 convolution_add_fusion.2
  136.6 1.6 fusion.57
  138.2 1.8 fusion.55
  141.3 2.7 convolution_add_fusion.2
  146.6 1.6 fusion.57
  148.2 1.8 fusion.55
  151.3 2.7 convolution_add_fusion.2
  156.6 1.6 fusion.57
  158.3 1.8 fusion.55
  161.3 2.7 convolution_add_fusion.2
  166.7 1.6 fusion.57
  168.3 1.8 fusion.55
  171.4 2.7 convolution_add_fusion.2
  176.7 1.6 fusion.57
  180.2 62.2 %psum.7 = f32[]{:T(128)} all-reduce(f32[]{:T(128)} %bitcast), channel_id=1, replica_groups=mesh['grp'=4,'comp'=16,'tp'=8] {'comp'}, use_global_device_ids=true, to_apply=%region_0.0 | all-reduce | flops 1 | bytes 8 | tf_op jit(solution)/shard_map/psum | solution.py:90
  243.1 1.3 maximum_multiply_fusion
  244.4 1.2 copy-done.2
  247.6 104.5 %reduce-scatter.2.cloned.1.call-done = f32[96,256]{1,0:T(8,128)} async-done(((f32[1536,256]{1,0:T(8,128)}), f32[96,256]{1,0:T(8,128)}) %reduce-scatter.2.cloned.1.call-update) | async-done | bytes 98320 | tf_op jit(solution)/shard_map/reduce_scatter | solution.py:105
  (109 shorter events, 38.6 us)
Async XLA Ops:
  7.2 89.3 %copy-start.3 = (bf16[256,1024]{1,0:T(8,128)(2,1)S(1)}, bf16[256,1024]{1,0:T(8,128)(2,1)}, u32[]{:S(2)}) copy-start(bf16[256,1024]{1,0:T(8,128)(2,1)} %param.10) | copy-start | bytes 1572868
  7.2 344.9 %reduce-scatter.2.cloned.1.call-start = ((), (), s32[]{:S(2)}) async-start(), calls=%async_computation.1 | async-start | bytes 1671168 | tf_op jit(solution)/shard_map/reduce_scatter | solution.py:105
  7.3 91.1 %copy-start.4 = (bf16[256,128]{1,0:T(8,128)(2,1)S(1)}, bf16[256,128]{1,0:T(8,128)(2,1)}, u32[]{:S(2)}) copy-start(bf16[256,128]{1,0:T(8,128)(2,1)} %param.11) | copy-start | bytes 196612
  9.3 89.9 %copy-start.5 = (bf16[256,128]{1,0:T(8,128)(2,1)S(1)}, bf16[256,128]{1,0:T(8,128)(2,1)}, u32[]{:S(2)}) copy-start(bf16[256,128]{1,0:T(8,128)(2,1)} %param.12) | copy-start | bytes 196612
  104.4 1.0 copy-start.1
  114.4 1.0 copy-start.1
  124.5 1.0 copy-start.1
  134.5 1.0 copy-start.1
  144.5 1.0 copy-start.1
  154.6 1.0 copy-start.1
  164.6 1.0 copy-start.1
  174.7 1.0 copy-start.1
  178.3 1.2 copy-start
  244.4 1.2 copy-start.2
Sparse Core Ops, SparseCore 0:
  244.5 107.5 reduce-scatter.1
where the time goes:
time: 363 us; the launch traced here: 360 us
  blocking collectives  149 us (41%)
  waiting for transfers between devices  104 us (29%)
  matrix products  64.2 us (18%)
  local copies, waits for them, and re-layouts  16.9 us (5%)
  between operations  16.1 us (4%)
  other arithmetic  8.86 us (2%)
    reduce_scatter x1, waiting for transfers between devices, shards(): summed = lax.psum_scatter(terms, 'comp', scatter_dimension=0, tiled=True)  104 us
    psum x1, blocking collectives, shards(): reward_sum = lax.psum(jnp.sum(rewards), 'comp')  62.2 us
    all_gather x1, blocking collectives, shards(): lax.all_gather(prompt_keys, 'comp', axis=0, tiled=True)  52.2 us
    all_gather x1, blocking collectives, shards(): lax.all_gather(prompt_values, 'comp', axis=0, tiled=True)  35 us
    dot_general x8, matrix products, one_head(): dvalue = jnp.dot(probs_half.T, cot_head, preferred_element_type=jnp.float32)  20.5 us
    dot_general x8, matrix products, head_terms(): jnp.dot(query_head, keys.T, preferred_element_type=jnp.float32) * scale  14.3 us
    dot_general x8, matrix products, one_head(): jnp.dot(dscores.T, query_head, preferred_element_type=jnp.float32) * scale  12.8 us
    dot_general x8, matrix products, one_head(): jnp.dot(dscores, key_group, preferred_element_type=jnp.float32) * scale  8.31 us
  transfers between devices with their start and end apart: 1, of which 1 were waited for; matrix products, arithmetic and copies ran while one was open for 1% of the time, Pallas kernels for 0%

commit v1 on v0

v1 whole, which is shorter than its diff:
```python
import math

import jax
import jax.numpy as jnp
from jax import lax
from jax.experimental import pallas as pl
from jax.experimental.pallas import tpu as pltpu
from jax.sharding import PartitionSpec as P

D = 128
HEADS = 8
ROWS = 256
SHARD = 96
PAIR = 2 * SHARD
HALF = 8 * SHARD
SPAN = 2 * HALF
KEYS = SPAN + ROWS
COLS = HEADS * ROWS
CHUNKS = SPAN // PAIR + 1
SCALE = D ** (-0.5)
EXP2_SCALE = SCALE * math.log2(math.e)
F32 = jnp.float32
BF16 = jnp.bfloat16
MESH = pl.DeviceIdType.MESH
NEAR = [(dx, dc) for dx in (2, 1, 3, 0) for dc in (0, 1) if (dx, dc) != (0, 0)]


def slot_of(dx, dc):
    return (dx % 4) * 2 + dc


def mm(a, b):
    return jnp.dot(a, b, preferred_element_type=F32)


def mm_t(a, b):
    return lax.dot_general(a, b, (((1,), (1,)), ((), ())), preferred_element_type=F32)


def kernel(
    q_hbm, ck_hbm, cv_hbm, pk_hbm, pv_hbm, up_hbm, reward_ref, length_ref,
    dq_hbm, dck_hbm, dcv_hbm, dpk_hbm, dpv_hbm,
    q_in, up_in, ck_in, cv_in, pk_in, pv_in,
    dq_out, dck_out, dcv_out, dpk_out, dpv_out,
    qs, cs, kv, kt, exps, dps, ps, dss, tops, sums, dots, factors, deltas,
    own, far_send, far_recv, near_send, near_recv, z_send, z_recv,
    reward_own, reward_z, reward_pair, reward_recv,
    in_sem, out_sem, near_ss, near_rs, far_ss, far_rs, zkv_ss, zkv_rs,
    rfar_ss, rfar_rs, rnear_ss, rnear_rs, rz_ss, rz_rs,
    rw_ss, rw_rs, rwz_ss, rwz_rs,
):
    grp = lax.axis_index("grp")
    comp = lax.axis_index("comp")
    tp = lax.axis_index("tp")
    core = comp % 2
    x = (comp // 2) % 4
    z = comp // 8

    def device(dz, dx, dc):
        zz = 1 - z if dz else z
        cc = 1 - core if dc else core
        return (grp, zz * 8 + ((x + dx) % 4) * 2 + cc, tp)

    partner = device(1, 0, 0)
    barrier = pltpu.get_barrier_semaphore()
    pl.semaphore_signal(barrier, inc=1, device_id=partner, device_id_type=MESH)
    for dx, dc in NEAR:
        pl.semaphore_signal(barrier, inc=1, device_id=device(0, dx, dc), device_id_type=MESH)

    loads = [
        pltpu.make_async_copy(src, dst, in_sem.at[i])
        for i, (src, dst) in enumerate(
            [(pk_hbm, pk_in), (pv_hbm, pv_in), (q_hbm, q_in), (ck_hbm, ck_in), (up_hbm, up_in), (cv_hbm, cv_in)]
        )
    ]
    for load in loads:
        load.start()
    loads[0].wait()
    loads[1].wait()
    kv[0, 0, :, :D] = pk_in[...]
    kv[0, 0, :, D:] = pv_in[...]
    reward_own[...] = jnp.full((1, D), reward_ref[0], F32)

    for load in loads[2:]:
        load.wait()
    valid = lax.broadcasted_iota(jnp.int32, (ROWS, D), 0) < length_ref[0]
    for h in range(HEADS):
        block = slice(h * D, (h + 1) * D)
        qs[h * ROWS : (h + 1) * ROWS, :] = q_in[:, block]
        upstream = up_in[:, block]
        cs[h * ROWS : (h + 1) * ROWS, :] = jnp.where(valid, upstream, jnp.zeros_like(upstream))

    def scores_of(keys, values, row, chunk, mask):
        count = keys.shape[0]

        def one_head(h, _):
            at = pl.ds(pl.multiple_of(h * ROWS, ROWS), ROWS)
            s = mm_t(keys, qs[at, :]) * EXP2_SCALE
            d = mm_t(values, cs[at, :])
            if mask is not None:
                s = jnp.where(mask, s, -1e30)
            top = jnp.max(s, axis=0, keepdims=True)
            e = jnp.exp2(s - top)
            exps[row : row + count, at] = e
            dps[row : row + count, at] = d
            tops[chunk : chunk + 1, at] = top
            sums[chunk : chunk + 1, at] = jnp.sum(e, axis=0, keepdims=True)
            dots[chunk : chunk + 1, at] = jnp.sum(e * d, axis=0, keepdims=True)
            return 0

        lax.fori_loop(0, HEADS, one_head, 0, unroll=2)

    def pair_scores(half, dx):
        block = kv[half, 2 * dx : 2 * dx + 2].reshape(PAIR, 2 * D)
        chunk = half * 4 + dx
        scores_of(block[:, :D], block[:, D:], chunk * PAIR, chunk, None)

    key_pos = lax.broadcasted_iota(jnp.int32, (ROWS, ROWS), 0)
    query_pos = lax.broadcasted_iota(jnp.int32, (ROWS, ROWS), 1)
    scores_of(ck_in[...], cv_in[...], SPAN, CHUNKS - 1, key_pos <= query_pos)

    pl.semaphore_wait(barrier, len(NEAR) + 1)

    def send(src, dst, ss, rs, to):
        copy = pltpu.make_async_remote_copy(
            src_ref=src, dst_ref=dst, send_sem=ss, recv_sem=rs, device_id=to, device_id_type=MESH
        )
        copy.start()
        return copy

    z_copy = send(kv.at[0, 0], kv.at[1, 0], zkv_ss, zkv_rs, partner)
    rz_copy = send(reward_own, reward_z, rwz_ss, rwz_rs, partner)
    pending = [z_copy, rz_copy]

    def spread(source, dest, ss, rs):
        copies = {}
        for i, (dx, dc) in enumerate(NEAR):
            there = slot_of(-dx, dc)
            copies[there] = send(source(dx, dc), dest(there), ss.at[i], rs.at[there], device(0, dx, dc))
            pending.append(copies[there])
        return copies

    near = spread(lambda dx, dc: kv.at[0, 0], lambda s: kv.at[0, s], near_ss, near_rs)
    near[1].wait_recv()
    pair_scores(0, 0)
    for dx in (1, 3, 2):
        near[2 * dx].wait_recv()
        near[2 * dx + 1].wait_recv()
        pair_scores(0, dx)

    z_copy.wait_recv()
    far = spread(lambda dx, dc: kv.at[1, 0], lambda s: kv.at[1, s], far_ss, far_rs)
    rz_copy.wait_recv()
    reward_pair[...] = reward_own[...] + reward_z[...]
    reward_copies = spread(lambda dx, dc: reward_pair, lambda s: reward_recv.at[s], rw_ss, rw_rs)

    far[1].wait_recv()
    pair_scores(1, 0)
    for dx in (1, 3, 2):
        far[2 * dx].wait_recv()
        far[2 * dx + 1].wait_recv()
        pair_scores(1, dx)

    total = reward_pair[...]
    for there, copy in reward_copies.items():
        copy.wait_recv()
        total = total + reward_recv[there]
    advantage = reward_own[...] - total / 16.0

    top = tops[0:CHUNKS, :]
    factor = jnp.exp2(top - jnp.max(top, axis=0, keepdims=True))
    inverse = 1.0 / jnp.sum(sums[0:CHUNKS, :] * factor, axis=0, keepdims=True)
    factors[0:CHUNKS, :] = factor * inverse
    deltas[...] = jnp.sum(dots[0:CHUNKS, :] * factor, axis=0, keepdims=True) * inverse

    def grads_of(row, count, chunk):
        def one_head(h, _):
            at = pl.ds(pl.multiple_of(h * ROWS, ROWS), ROWS)
            p = exps[row : row + count, at] * factors[chunk : chunk + 1, at]
            ps[0:count, at] = p.astype(BF16)
            dss[row : row + count, at] = (p * (dps[row : row + count, at] - deltas[:, at])).astype(BF16)
            return 0

        lax.fori_loop(0, HEADS, one_head, 0, unroll=2)
        dkey = mm(dss[row : row + count, :], qs[...]) * (advantage * SCALE)
        dvalue = mm(ps[0:count, :], cs[...]) * advantage
        return dkey, dvalue

    def terms(half, sends, ss, rs, recv):
        copies = {}
        order = {pair: i for i, pair in enumerate(NEAR)}
        for dx in (2, 1, 3, 0):
            chunk = half * 4 + dx
            dkey, dvalue = grads_of(chunk * PAIR, PAIR, chunk)
            for dc in (0, 1):
                rows = slice(dc * SHARD, (dc + 1) * SHARD)
                if (dx, dc) == (0, 0):
                    own[half, :, :D] = dkey[rows]
                    own[half, :, D:] = dvalue[rows]
                    continue
                here, there = slot_of(dx, dc), slot_of(-dx, dc)
                sends[here, :, :D] = dkey[rows].astype(BF16)
                sends[here, :, D:] = dvalue[rows].astype(BF16)
                i = order[(dx, dc)]
                copies[there] = send(
                    sends.at[here], recv.at[there], ss.at[i], rs.at[there], device(0, dx, dc)
                )
                pending.append(copies[there])
        return copies

    def collect(half, copies, recv):
        result = own[half]
        for there, copy in copies.items():
            copy.wait_recv()
            result = result + recv[there].astype(F32)
        return result

    far_terms = terms(1, far_send, rfar_ss, rfar_rs, far_recv)
    near_terms = terms(0, near_send, rnear_ss, rnear_rs, near_recv)

    z_send[...] = collect(1, far_terms, far_recv).astype(BF16)
    z_terms = send(z_send, z_recv, rz_ss, rz_rs, partner)
    pending.append(z_terms)

    dkey, dvalue = grads_of(SPAN, ROWS, CHUNKS - 1)
    dck_out[...] = dkey.astype(BF16)
    dcv_out[...] = dvalue.astype(BF16)
    for half in (0, 1):
        for s in range(8):
            at = half * HALF + s * SHARD
            kt[at : at + SHARD, :] = kv[half, s, :, :D]
    kt[SPAN:, :] = ck_in[...]
    keys_t = kt[...].T
    for h in range(HEADS):
        dquery = mm(keys_t, dss[:, h * ROWS : (h + 1) * ROWS])
        dq_out[:, h * D : (h + 1) * D] = (dquery.T * (advantage * SCALE)).astype(BF16)
    stores = [
        pltpu.make_async_copy(dq_out, dq_hbm, out_sem.at[0]),
        pltpu.make_async_copy(dck_out, dck_hbm, out_sem.at[1]),
        pltpu.make_async_copy(dcv_out, dcv_hbm, out_sem.at[2]),
    ]
    for store in stores:
        store.start()

    near_sum = collect(0, near_terms, near_recv)
    z_terms.wait_recv()
    result = near_sum + z_recv[...].astype(F32)
    dpk_out[...] = result[:, :D].astype(BF16)
    dpv_out[...] = result[:, D:].astype(BF16)
    last = [
        pltpu.make_async_copy(dpk_out, dpk_hbm, out_sem.at[3]),
        pltpu.make_async_copy(dpv_out, dpv_hbm, out_sem.at[4]),
    ]
    for store in last:
        store.start()
    for copy in pending:
        copy.wait_send()
    for store in stores + last:
        store.wait()


def shards(queries, comp_keys, comp_values, prompt_keys, prompt_values, upstream, rewards, lengths):
    hbm = pl.BlockSpec(memory_space=pl.ANY)
    smem = pl.BlockSpec(memory_space=pltpu.SMEM)
    vmem = pltpu.VMEM
    dma = pltpu.SemaphoreType.DMA
    return pl.pallas_call(
        kernel,
        name="attention_backward",
        out_shape=[
            jax.ShapeDtypeStruct((ROWS, HEADS * D), BF16),
            jax.ShapeDtypeStruct((ROWS, D), BF16),
            jax.ShapeDtypeStruct((ROWS, D), BF16),
            jax.ShapeDtypeStruct((SHARD, D), BF16),
            jax.ShapeDtypeStruct((SHARD, D), BF16),
        ],
        in_specs=[hbm] * 6 + [smem] * 2,
        out_specs=[hbm] * 5,
        scratch_shapes=[
            vmem((ROWS, HEADS * D), BF16),
            vmem((ROWS, HEADS * D), BF16),
            vmem((ROWS, D), BF16),
            vmem((ROWS, D), BF16),
            vmem((SHARD, D), BF16),
            vmem((SHARD, D), BF16),
            vmem((ROWS, HEADS * D), BF16),
            vmem((ROWS, D), BF16),
            vmem((ROWS, D), BF16),
            vmem((SHARD, D), BF16),
            vmem((SHARD, D), BF16),
            vmem((COLS, D), BF16),
            vmem((COLS, D), BF16),
            vmem((2, 8, SHARD, 2 * D), BF16),
            vmem((KEYS, D), BF16),
            vmem((KEYS, COLS), F32),
            vmem((KEYS, COLS), F32),
            vmem((ROWS, COLS), BF16),
            vmem((KEYS, COLS), BF16),
            vmem((16, COLS), F32),
            vmem((16, COLS), F32),
            vmem((16, COLS), F32),
            vmem((16, COLS), F32),
            vmem((1, COLS), F32),
            vmem((2, SHARD, 2 * D), F32),
            vmem((8, SHARD, 2 * D), BF16),
            vmem((8, SHARD, 2 * D), BF16),
            vmem((8, SHARD, 2 * D), BF16),
            vmem((8, SHARD, 2 * D), BF16),
            vmem((SHARD, 2 * D), BF16),
            vmem((SHARD, 2 * D), BF16),
            vmem((1, D), F32),
            vmem((1, D), F32),
            vmem((1, D), F32),
            vmem((8, 1, D), F32),
            dma((6,)),
            dma((5,)),
            dma((7,)),
            dma((8,)),
            dma((7,)),
            dma((8,)),
            dma,
            dma,
            dma((7,)),
            dma((8,)),
            dma((7,)),
            dma((8,)),
            dma,
            dma,
            dma((7,)),
            dma((8,)),
            dma,
            dma,
        ],
        compiler_params=pltpu.CompilerParams(
            collective_id=0, has_side_effects=True, vmem_limit_bytes=58 * 2**20
        ),
    )(queries, comp_keys, comp_values, prompt_keys, prompt_values, upstream, rewards, lengths)


def solution(mesh):
    rows = P(("grp", "comp"), "tp")
    scalars = P(("grp", "comp"))
    return jax.shard_map(
        shards, mesh=mesh, in_specs=(rows,) * 6 + (scalars,) * 2, out_specs=(rows,) * 5, check_vma=False
    )
```

time: 363 us -> 59.5 us (0.16)
  blocking collectives: 149 us -> 0 us
  waiting for transfers between devices: 104 us -> 0 us
  matrix products: 64.2 us -> 0 us
  Pallas kernels: 0 us -> 52.3 us
  between operations: 16.1 us -> 1.95 us
  local copies, waits for them, and re-layouts: 16.9 us -> 4.86 us
  other arithmetic: 8.86 us -> 0 us
    reduce_scatter x1 -> x0, waiting for transfers between devices: 104 us -> none  [shards(): summed = lax.psum_scatter(terms, 'comp', scatter_dimension=0, tiled=True)]
    all_gather x2 -> x0, blocking collectives: 87.2 us -> none  [the longest x1 52.2 us: shards(): lax.all_gather(prompt_keys, 'comp', axis=0, tiled=True)]
    dot_general x48 -> x0, matrix products: 64.2 us -> none  [the longest x8 20.5 us: one_head(): dvalue = jnp.dot(probs_half.T, cot_head, preferred_element_type=jnp.float32)]
    psum x1 -> x0, blocking collectives: 62.2 us -> none  [shards(): reward_sum = lax.psum(jnp.sum(rewards), 'comp')]
    pallas_call x0 -> x1, Pallas kernels: none -> 52.3 us  [shards(): pl.pallas_call(kernel, name='attention_backward', out_shape=[jax.ShapeDty...]
    dynamic_slice x16 -> x0, local copies, waits for them, and re-layouts: 7.7 us -> none  [one_group(): lax.scan(one_head, (empty, empty), (query_group, cot_group))]
    reduce_sum x16 -> x0, other arithmetic: 4.16 us -> none  [the longest x8 3.24 us: head_terms(): lse = top + jnp.log(jnp.sum(jnp.exp(scores - top), axis=1, keepdims=True))]
  transfers between devices with their start and end apart: 1 -> 0, of which waited for: 1 -> 0; matrix products, arithmetic and copies ran while one was open for 1% -> 0% of each run, Pallas kernels for 0% -> 0%
where the time goes in v1:
time: 59.5 us; the launch traced here: 59.1 us
  Pallas kernels  52.3 us (88%)
  local copies, waits for them, and re-layouts  4.86 us (8%)
  between operations  1.95 us (3%)
    pallas_call x1, Pallas kernels, shards(): pl.pallas_call(kernel, name='attention_backward', out_shape=[jax.ShapeDty...  52.3 us
    unnamed x13, local copies, waits for them, and re-layouts  4.86 us

profile of v1, /device:TPU:1, one launch (start us, length us, event | category | flops | bytes accessed | tf_op | source)
XLA Modules:
  0.0 59.1 jit_solution(17731222478762086659)
XLA Ops:
  1.9 52.3 %attention_backward.1 = (bf16[256,1024]{1,0:T(8,128)(2,1)}, bf16[256,128]{1,0:T(8,128)(2,1)}, bf16[256,128]{1,0:T(8,128)(2,1)}, bf16[96,128]{1,0:T(8,128)(2,1)}, bf16[96,128]{1,0:T(8,128)(2,1)}) custom-call(bf16[256,1024]{1,0:T(8,128)(2,1)} %q_hbm.1, bf16[256,128]{1,0:T(8,128)(2,1)} %ck_hbm.1, bf16[256,128]{1,0:T(8,128)(2,1)} %cv_hbm.1, ...), custom_call_target="tpu_custom_call" | custom-call | tf_op jit(solution)/shard_map/attention_backward/pallas_call | solution.py:267
  54.3 0.0 copy-start.1
  54.3 1.9 %copy.20 = bf16[256,1024]{1,0:T(8,128)(2,1)} copy(bf16[256,1024]{1,0:T(8,128)(2,1)} %get-tuple-element.10) | data formatting | bytes 1048576
  56.2 0.0 copy-done.1
  56.2 0.0 copy-start
  56.2 0.6 %copy.21 = bf16[256,128]{1,0:T(8,128)(2,1)} copy(bf16[256,128]{1,0:T(8,128)(2,1)S(1)} %copy-done.1) | data formatting | bytes 131072
  56.8 0.2 copy-done
  57.0 0.0 copy-start.3
  57.0 0.6 %copy.22 = bf16[256,128]{1,0:T(8,128)(2,1)} copy(bf16[256,128]{1,0:T(8,128)(2,1)S(1)} %copy-done) | data formatting | bytes 131072
  57.7 0.1 copy-done.3
  57.8 0.0 copy-start.2
  57.8 0.6 %copy.23 = bf16[96,128]{1,0:T(8,128)(2,1)} copy(bf16[96,128]{1,0:T(8,128)(2,1)S(1)} %copy-done.3) | data formatting | bytes 49152
  58.4 0.1 copy-done.2
  58.5 0.6 %copy.24 = bf16[96,128]{1,0:T(8,128)(2,1)} copy(bf16[96,128]{1,0:T(8,128)(2,1)S(1)} %copy-done.2) | data formatting | bytes 49152
Async XLA Ops:
  54.3 1.9 %copy-start.1 = (bf16[256,128]{1,0:T(8,128)(2,1)S(1)}, bf16[256,128]{1,0:T(8,128)(2,1)}, u32[]{:S(2)}) copy-start(bf16[256,128]{1,0:T(8,128)(2,1)} %get-tuple-element.11) | copy-start | bytes 196612
  56.2 0.9 %copy-start = (bf16[256,128]{1,0:T(8,128)(2,1)S(1)}, bf16[256,128]{1,0:T(8,128)(2,1)}, u32[]{:S(2)}) copy-start(bf16[256,128]{1,0:T(8,128)(2,1)} %get-tuple-element.12) | copy-start | bytes 196612
  57.0 0.7 %copy-start.3 = (bf16[96,128]{1,0:T(8,128)(2,1)S(1)}, bf16[96,128]{1,0:T(8,128)(2,1)}, u32[]{:S(2)}) copy-start(bf16[96,128]{1,0:T(8,128)(2,1)} %get-tuple-element.13) | copy-start | bytes 73732
  57.8 0.7 %copy-start.2 = (bf16[96,128]{1,0:T(8,128)(2,1)S(1)}, bf16[96,128]{1,0:T(8,128)(2,1)}, u32[]{:S(2)}) copy-start(bf16[96,128]{1,0:T(8,128)(2,1)} %get-tuple-element.14) | copy-start | bytes 73732

commit v2 on v1

v2 whole, which is shorter than its diff:
```python
import math

import jax
import jax.numpy as jnp
from jax import lax
from jax.experimental import pallas as pl
from jax.experimental.pallas import tpu as pltpu
from jax.sharding import PartitionSpec as P

D = 128
HEADS = 8
ROWS = 256
SHARD = 96
HALF = 8 * SHARD
SPAN = 2 * HALF
KEYS = SPAN + ROWS
OWN_CHUNK = 6
CHUNKS = 7
COLS = HEADS * ROWS
QUAD = 4 * SHARD
FIRST, REST, ALL = (0, 1), (1, 4), (0, 4)
SCALE = D ** (-0.5)
EXP2_SCALE = SCALE * math.log2(math.e)
F32 = jnp.float32
BF16 = jnp.bfloat16
MESH = pl.DeviceIdType.MESH
PEERS = (2, 1, 3)
KEY, VALUE = 0, 1


def mm(a, b):
    return jnp.dot(a, b, preferred_element_type=F32)


def mm_t(a, b):
    return lax.dot_general(a, b, (((1,), (1,)), ((), ())), preferred_element_type=F32)


def kernel(
    q_hbm, ck_hbm, cv_hbm, pk_hbm, pv_hbm, up_hbm, reward_hbm, length_hbm,
    dq_out, dckv_out, dpkv_out,
    q_in, up_in, ck_in, cv_in, pk_in, pv_in, reward_ref, length_ref,
    qs, cs, kv, kt, exps, dps, ps, dss, tops, sums, dots, factors, deltas,
    held, pair_send, pair_recv, row_send, row_recv, z_send, z_recv,
    reward_own, reward_z, reward_pair, reward_quad, reward_sib, reward_recv,
    in_sem, kv_ss, kv_rs, row_ss, row_rs, sum_ss, sum_rs, pair_ss, pair_rs, misc_ss, misc_rs,
):
    grp = lax.axis_index("grp")
    comp = lax.axis_index("comp")
    tp = lax.axis_index("tp")
    core = comp % 2
    x = (comp // 2) % 4
    z = comp // 8
    partner = (grp, (1 - z) * 8 + x * 2 + core, tp)
    sibling = (grp, z * 8 + x * 2 + 1 - core, tp)
    row = {dx: (grp, z * 8 + ((x + dx) % 4) * 2 + core, tp) for dx in PEERS}

    barrier = pltpu.get_barrier_semaphore()
    for peer in (partner, *row.values(), sibling):
        pl.semaphore_signal(barrier, inc=1, device_id=peer, device_id_type=MESH)

    loads = [
        pltpu.make_async_copy(src, dst, in_sem.at[i])
        for i, (src, dst) in enumerate(
            [
                (pk_hbm, pk_in), (pv_hbm, pv_in), (reward_hbm, reward_ref), (length_hbm, length_ref),
                (q_hbm, q_in), (ck_hbm, ck_in), (up_hbm, up_in), (cv_hbm, cv_in),
            ]
        )
    ]
    for load in loads:
        load.start()
    for load in loads[:4]:
        load.wait()
    kv[0, 0, 0, :, :D] = pk_in[...]
    kv[0, 0, 0, :, D:] = pv_in[...]
    reward_own[...] = jnp.full((1, D), reward_ref[0], F32)

    pl.semaphore_wait(barrier, 5)

    pending = []

    def send(src, dst, ss, rs, to):
        copy = pltpu.make_async_remote_copy(
            src_ref=src, dst_ref=dst, send_sem=ss, recv_sem=rs, device_id=to, device_id_type=MESH
        )
        copy.start()
        pending.append(copy)
        return copy

    def across(src, dst, i):
        return send(src, dst, misc_ss.at[i], misc_rs.at[i], partner)

    def spread(half):
        own = kv.at[half, 0, 0]
        along = {
            (4 - dx) % 4: send(
                own, kv.at[half, 0, (4 - dx) % 4], kv_ss.at[half, 0, dx], kv_rs.at[half, 0, (4 - dx) % 4], row[dx]
            )
            for dx in PEERS
        }
        beside = {0: send(own, kv.at[half, 1, 0], kv_ss.at[half, 1, 0], kv_rs.at[half, 1, 0], sibling)}
        return along, beside

    def forward(half, along, beside):
        for dx in (1, 3, 2):
            along[dx].wait_recv()
            beside[dx] = send(
                kv.at[half, 0, dx], kv.at[half, 1, dx], kv_ss.at[half, 1, dx], kv_rs.at[half, 1, dx], sibling
            )

    def scores_of(keys, values, at_row, chunk, mask=None):
        rows = slice(at_row, at_row + keys.shape[0])
        for h in range(HEADS):
            at = slice(h * ROWS, (h + 1) * ROWS)
            s = mm_t(keys, qs[at, :]) * EXP2_SCALE
            d = mm_t(values, cs[at, :])
            if mask is not None:
                s = jnp.where(mask, s, -1e30)
            top = jnp.max(s, axis=0, keepdims=True)
            e = jnp.exp2(s - top)
            exps[rows, at] = e
            dps[rows, at] = d
            tops[chunk : chunk + 1, at] = top
            sums[chunk : chunk + 1, at] = jnp.sum(e, axis=0, keepdims=True)
            dots[chunk : chunk + 1, at] = jnp.sum(e * d, axis=0, keepdims=True)

    def prompt_scores(half, parity, part, chunk):
        first, last = part
        block = kv[half, parity, first:last].reshape((last - first) * SHARD, 2 * D)
        scores_of(block[:, :D], block[:, D:], half * HALF + parity * QUAD + first * SHARD, chunk)

    kv_z = across(kv.at[0, 0, 0], kv.at[1, 0, 0], 0)
    reward_across = across(reward_own, reward_z, 1)
    along, beside = spread(0)

    for load in loads[4:]:
        load.wait()
    valid = lax.broadcasted_iota(jnp.int32, (ROWS, D), 0) < length_ref[0]
    for h in range(HEADS):
        block = slice(h * D, (h + 1) * D)
        qs[h * ROWS : (h + 1) * ROWS, :] = q_in[:, block]
        upstream = up_in[:, block]
        cs[h * ROWS : (h + 1) * ROWS, :] = jnp.where(valid, upstream, jnp.zeros_like(upstream))

    key_pos = lax.broadcasted_iota(jnp.int32, (ROWS, ROWS), 0)
    query_pos = lax.broadcasted_iota(jnp.int32, (ROWS, ROWS), 1)
    scores_of(ck_in[...], cv_in[...], SPAN, OWN_CHUNK, key_pos <= query_pos)

    forward(0, along, beside)
    prompt_scores(0, 0, ALL, 0)

    kv_z.wait_recv()
    near_beside = beside
    along, beside = spread(1)
    reward_across.wait_recv()
    reward_pair[...] = reward_own[...] + reward_z[...]
    reward_along = {
        (4 - dx) % 4: send(
            reward_pair, reward_recv.at[(4 - dx) % 4], row_ss.at[dx], row_rs.at[(4 - dx) % 4], row[dx]
        )
        for dx in PEERS
    }
    for copy in near_beside.values():
        copy.wait_recv()
    prompt_scores(0, 1, ALL, 1)
    prompt_scores(1, 0, FIRST, 2)
    beside[0].wait_recv()
    prompt_scores(1, 1, FIRST, 3)
    forward(1, along, beside)
    total = reward_pair[...]
    for dx, copy in reward_along.items():
        copy.wait_recv()
        total = total + reward_recv[dx]
    reward_quad[...] = total
    reward_beside = send(reward_quad, reward_sib, misc_ss.at[2], misc_rs.at[2], sibling)
    prompt_scores(1, 0, REST, 4)
    for dx in (1, 3, 2):
        beside[dx].wait_recv()
    prompt_scores(1, 1, REST, 5)

    reward_beside.wait_recv()
    advantage = reward_own[...] - (reward_quad[...] + reward_sib[...]) / 16.0

    top = tops[0:CHUNKS, :]
    factor = jnp.exp2(top - jnp.max(top, axis=0, keepdims=True))
    inverse = 1.0 / jnp.sum(sums[0:CHUNKS, :] * factor, axis=0, keepdims=True)
    factors[0:CHUNKS, :] = factor * inverse
    deltas[...] = jnp.sum(dots[0:CHUNKS, :] * factor, axis=0, keepdims=True) * inverse

    def value_terms(at_row, chunks, room):
        count = sum(size for _, size in chunks)
        for h in range(HEADS):
            at = slice(h * ROWS, (h + 1) * ROWS)
            start = 0
            for chunk, size in chunks:
                rows = slice(at_row + start, at_row + start + size)
                p = exps[rows, at] * factors[chunk : chunk + 1, at]
                ps[room, start : start + size, at] = p.astype(BF16)
                start += size
        return mm(ps[room, 0:count, :], cs[...]) * advantage

    def key_terms(at_row, chunks):
        count = sum(size for _, size in chunks)
        for h in range(HEADS):
            at = slice(h * ROWS, (h + 1) * ROWS)
            start = 0
            for chunk, size in chunks:
                rows = slice(at_row + start, at_row + start + size)
                p = exps[rows, at] * factors[chunk : chunk + 1, at]
                dss[rows, at] = (p * (dps[rows, at] - deltas[:, at])).astype(BF16)
                start += size
        return mm(dss[at_row : at_row + count, :], qs[...]) * (advantage * SCALE)

    def to_sibling(half, kind, block):
        for dx in range(4):
            pair_send[half, kind, dx] = block[dx * SHARD : (dx + 1) * SHARD].astype(BF16)
        return send(
            pair_send.at[half, kind], pair_recv.at[half, kind], pair_ss.at[half, kind], pair_rs.at[half, kind], sibling
        )

    def along_row(half, kind, copy):
        copy.wait_recv()
        copies = {}
        for dx in PEERS:
            both = held[half, kind, dx * SHARD : (dx + 1) * SHARD] + pair_recv[half, kind, dx].astype(F32)
            row_send[half, kind, dx] = both.astype(BF16)
            there = (4 - dx) % 4
            copies[there] = send(
                row_send.at[half, kind, dx], row_recv.at[half, kind, there],
                sum_ss.at[half, kind, dx], sum_rs.at[half, kind, there], row[dx],
            )
        return copies

    def collect(half, kind, copies):
        result = held[half, kind, 0:SHARD] + pair_recv[half, kind, 0].astype(F32)
        for dx, copy in copies.items():
            copy.wait_recv()
            result = result + row_recv[half, kind, dx].astype(F32)
        return result

    def to_partner(kind, copies):
        z_send[kind] = collect(1, kind, copies).astype(BF16)
        return across(z_send.at[kind], z_recv.at[kind], 3 + kind)

    even, odd = ((2, SHARD), (4, QUAD - SHARD)), ((3, SHARD), (5, QUAD - SHARD))
    value_pair = to_sibling(1, VALUE, value_terms(HALF + QUAD, odd, 0))
    held[1, VALUE] = value_terms(HALF, even, 1)
    key_pair = to_sibling(1, KEY, key_terms(HALF + QUAD, odd))
    value_rows = along_row(1, VALUE, value_pair)
    held[1, KEY] = key_terms(HALF, even)
    key_rows = along_row(1, KEY, key_pair)

    for half in (0, 1):
        for parity in (0, 1):
            start = half * HALF + parity * QUAD
            kt[start : start + QUAD, :] = kv[half, parity].reshape(QUAD, 2 * D)[:, :D]
    kt[SPAN:, :] = ck_in[...]
    dckv_out[:, D:] = value_terms(SPAN, ((OWN_CHUNK, ROWS),), 0).astype(BF16)
    dckv_out[:, :D] = key_terms(SPAN, ((OWN_CHUNK, ROWS),)).astype(BF16)
    z_value = to_partner(VALUE, value_rows)
    z_key = to_partner(KEY, key_rows)

    near_value_pair = to_sibling(0, VALUE, value_terms(QUAD, ((1, QUAD),), 0))
    near_key_pair = to_sibling(0, KEY, key_terms(QUAD, ((1, QUAD),)))
    held[0, VALUE] = value_terms(0, ((0, QUAD),), 1)
    held[0, KEY] = key_terms(0, ((0, QUAD),))
    near_value_rows = along_row(0, VALUE, near_value_pair)
    near_key_rows = along_row(0, KEY, near_key_pair)

    keys_t = kt[...].T
    for h in range(HEADS):
        dquery = mm(keys_t, dss[:, h * ROWS : (h + 1) * ROWS])
        dq_out[:, h * D : (h + 1) * D] = (dquery.T * (advantage * SCALE)).astype(BF16)

    near_value = collect(0, VALUE, near_value_rows)
    near_key = collect(0, KEY, near_key_rows)
    z_value.wait_recv()
    dpkv_out[:, D:] = (near_value + z_recv[VALUE].astype(F32)).astype(BF16)
    z_key.wait_recv()
    dpkv_out[:, :D] = (near_key + z_recv[KEY].astype(F32)).astype(BF16)
    for copy in pending:
        copy.wait_send()


def shards(queries, comp_keys, comp_values, prompt_keys, prompt_values, upstream, rewards, lengths):
    hbm = pl.BlockSpec(memory_space=pl.ANY)
    vmem = pltpu.VMEM
    dma = pltpu.SemaphoreType.DMA
    dquery, dcomp, dprompt = pl.pallas_call(
        kernel,
        name="attention_backward",
        out_shape=[
            vmem((ROWS, HEADS * D), BF16),
            vmem((ROWS, 2 * D), BF16),
            vmem((SHARD, 2 * D), BF16),
        ],
        in_specs=[hbm] * 8,
        out_specs=[pl.BlockSpec(memory_space=vmem)] * 3,
        scratch_shapes=[
            vmem((ROWS, HEADS * D), BF16),
            vmem((ROWS, HEADS * D), BF16),
            vmem((ROWS, D), BF16),
            vmem((ROWS, D), BF16),
            vmem((SHARD, D), BF16),
            vmem((SHARD, D), BF16),
            pltpu.SMEM((1,), F32),
            pltpu.SMEM((1,), jnp.int32),
            vmem((COLS, D), BF16),
            vmem((COLS, D), BF16),
            vmem((2, 2, 4, SHARD, 2 * D), BF16),
            vmem((KEYS, D), BF16),
            vmem((KEYS, COLS), F32),
            vmem((KEYS, COLS), F32),
            vmem((2, QUAD, COLS), BF16),
            vmem((KEYS, COLS), BF16),
            vmem((8, COLS), F32),
            vmem((8, COLS), F32),
            vmem((8, COLS), F32),
            vmem((8, COLS), F32),
            vmem((1, COLS), F32),
            vmem((2, 2, QUAD, D), F32),
            vmem((2, 2, 4, SHARD, D), BF16),
            vmem((2, 2, 4, SHARD, D), BF16),
            vmem((2, 2, 4, SHARD, D), BF16),
            vmem((2, 2, 4, SHARD, D), BF16),
            vmem((2, SHARD, D), BF16),
            vmem((2, SHARD, D), BF16),
            vmem((1, D), F32),
            vmem((1, D), F32),
            vmem((1, D), F32),
            vmem((1, D), F32),
            vmem((1, D), F32),
            vmem((4, 1, D), F32),
            dma((8,)),
            dma((2, 2, 4)),
            dma((2, 2, 4)),
            dma((4,)),
            dma((4,)),
            dma((2, 2, 4)),
            dma((2, 2, 4)),
            dma((2, 2)),
            dma((2, 2)),
            dma((6,)),
            dma((6,)),
        ],
        compiler_params=pltpu.CompilerParams(
            collective_id=0, has_side_effects=True, vmem_limit_bytes=56 * 2**20
        ),
    )(queries, comp_keys, comp_values, prompt_keys, prompt_values, upstream, rewards, lengths)
    return dquery, dcomp[:, :D], dcomp[:, D:], dprompt[:, :D], dprompt[:, D:]


def solution(mesh):
    rows = P(("grp", "comp"), "tp")
    scalars = P(("grp", "comp"))
    return jax.shard_map(
        shards, mesh=mesh, in_specs=(rows,) * 6 + (scalars,) * 2, out_specs=(rows,) * 5, check_vma=False
    )
```

time: 59.5 us -> 51.7 us (0.87)
  Pallas kernels: 52.3 us -> 47.6 us
  local copies, waits for them, and re-layouts: 4.86 us -> 2.08 us
    pallas_call x1, Pallas kernels: 52.3 us -> 47.6 us  [shards(): pl.pallas_call(kernel, name='attention_backward', out_shape=[vmem((ROWS,...]
    unnamed x13 -> x1, local copies, waits for them, and re-layouts: 4.86 us -> 0.8 us
    slice x0 -> x2, local copies, waits for them, and re-layouts: none -> 1.28 us  [shards(): return (dquery, dcomp[:, :D], dcomp[:, D:], dprompt[:, :D], dprompt[:, D:])]
where the time goes in v2:
time: 51.7 us; the launch traced here: 51.6 us
  Pallas kernels  47.6 us (92%)
  local copies, waits for them, and re-layouts  2.08 us (4%)
  between operations  1.93 us (4%)
    pallas_call x1, Pallas kernels, shards(): pl.pallas_call(kernel, name='attention_backward', out_shape=[vmem((ROWS,...  47.6 us
    slice x2, local copies, waits for them, and re-layouts, shards(): return (dquery, dcomp[:, :D], dcomp[:, D:], dprompt[:, :D], dprompt[:, D:])  1.28 us

profile of v2, /device:TPU:1, one launch (start us, length us, event | category | flops | bytes accessed | tf_op | source)
XLA Modules:
  0.0 51.6 jit_solution(16055942029555055096)
XLA Ops:
  1.9 47.6 %attention_backward.1 = (bf16[256,1024]{1,0:T(8,128)(2,1)S(1)}, bf16[256,256]{1,0:T(8,128)(2,1)S(1)}, bf16[96,256]{1,0:T(8,128)(2,1)S(1)}) custom-call(bf16[256,1024]{1,0:T(8,128)(2,1)} %q_hbm.1, bf16[256,128]{1,0:T(8,128)(2,1)} %ck_hbm.1, bf16[256,128]{1,0:T(8,128)(2,1)} %cv_hbm.1, bf16[96,128]{1,0:T(8,128)(2,1)} %pk_hbm.1, bf16[96,128]{1,0:T(8,128)(2,1)} %pv_hbm.1, ...), custom_call_target="tpu_custom_call" | custom-call | tf_op jit(solution)/shard_map/attention_backward/pallas_call | solution.py:290
  49.5 0.8 %copy.14 = bf16[256,1024]{1,0:T(8,128)(2,1)} copy(bf16[256,1024]{1,0:T(8,128)(2,1)S(1)} %get-tuple-element.15) | data formatting | bytes 1048576
  50.3 0.6 %fusion.1 = (bf16[96,128]{1,0:T(8,128)(2,1)}, bf16[96,128]{1,0:T(8,128)(2,1)}) fusion(bf16[96,256]{1,0:T(8,128)(2,1)S(1)} %get-tuple-element.10), kind=kLoop, calls=%fused_computation.1 | loop fusion | bytes 98304 | tf_op jit(solution)/shard_map/slice | solution.py:351
  50.9 0.7 %fusion = (bf16[256,128]{1,0:T(8,128)(2,1)}, bf16[256,128]{1,0:T(8,128)(2,1)}) fusion(bf16[256,256]{1,0:T(8,128)(2,1)S(1)} %get-tuple-element.9), kind=kLoop, calls=%fused_computation | loop fusion | bytes 262144 | tf_op jit(solution)/shard_map/slice | solution.py:351

commit v3 on v2

--- a/solution.py
+++ b/solution.py
@@ -188,36 +188,39 @@
     factors[0:CHUNKS, :] = factor * inverse
     deltas[...] = jnp.sum(dots[0:CHUNKS, :] * factor, axis=0, keepdims=True) * inverse
 
-    def value_terms(at_row, chunks, room):
-        count = sum(size for _, size in chunks)
+    def value_terms(at_row, count, chunk, room):
+        rows = slice(at_row, at_row + count)
         for h in range(HEADS):
             at = slice(h * ROWS, (h + 1) * ROWS)
-            start = 0
-            for chunk, size in chunks:
-                rows = slice(at_row + start, at_row + start + size)
-                p = exps[rows, at] * factors[chunk : chunk + 1, at]
-                ps[room, start : start + size, at] = p.astype(BF16)
-                start += size
+            ps[room, 0:count, at] = (exps[rows, at] * factors[chunk : chunk + 1, at]).astype(BF16)
         return mm(ps[room, 0:count, :], cs[...]) * advantage
 
-    def key_terms(at_row, chunks):
-        count = sum(size for _, size in chunks)
+    def key_terms(at_row, count, chunk, room):
+        rows = slice(at_row, at_row + count)
         for h in range(HEADS):
             at = slice(h * ROWS, (h + 1) * ROWS)
-            start = 0
-            for chunk, size in chunks:
-                rows = slice(at_row + start, at_row + start + size)
-                p = exps[rows, at] * factors[chunk : chunk + 1, at]
-                dss[rows, at] = (p * (dps[rows, at] - deltas[:, at])).astype(BF16)
-                start += size
-        return mm(dss[at_row : at_row + count, :], qs[...]) * (advantage * SCALE)
-
-    def to_sibling(half, kind, block):
-        for dx in range(4):
-            pair_send[half, kind, dx] = block[dx * SHARD : (dx + 1) * SHARD].astype(BF16)
+            p = exps[rows, at] * factors[chunk : chunk + 1, at]
+            dss[rows, at] = (p * (dps[rows, at] - deltas[:, at])).astype(BF16)
+        return mm(dss[rows, :], qs[...]) * (advantage * SCALE)
+
+    terms = {KEY: key_terms, VALUE: value_terms}
+
+    def to_sibling(half, kind, part, chunk):
+        first, last = part
+        start = half * HALF + QUAD + first * SHARD
+        block = terms[kind](start, (last - first) * SHARD, chunk, 0)
+        for dx in range(first, last):
+            pair_send[half, kind, dx] = block[(dx - first) * SHARD : (dx - first + 1) * SHARD].astype(BF16)
+        i = 1 if first else 0
         return send(
-            pair_send.at[half, kind], pair_recv.at[half, kind], pair_ss.at[half, kind], pair_rs.at[half, kind], sibling
+            pair_send.at[half, kind, pl.ds(first, last - first)], pair_recv.at[half, kind, pl.ds(first, last - first)],
+            pair_ss.at[half, kind, i], pair_rs.at[half, kind, i], sibling,
         )
+
+    def hold(half, kind, part, chunk):
+        first, last = part
+        start = half * HALF + first * SHARD
+        held[half, kind, first * SHARD : last * SHARD] = terms[kind](start, (last - first) * SHARD, chunk, 1)
 
     def along_row(half, kind, copy):
         copy.wait_recv()
@@ -243,31 +246,36 @@
         z_send[kind] = collect(1, kind, copies).astype(BF16)
         return across(z_send.at[kind], z_recv.at[kind], 3 + kind)
 
-    even, odd = ((2, SHARD), (4, QUAD - SHARD)), ((3, SHARD), (5, QUAD - SHARD))
-    value_pair = to_sibling(1, VALUE, value_terms(HALF + QUAD, odd, 0))
-    held[1, VALUE] = value_terms(HALF, even, 1)
-    key_pair = to_sibling(1, KEY, key_terms(HALF + QUAD, odd))
+    value_pair = to_sibling(1, VALUE, REST, 5)
+    hold(1, VALUE, REST, 4)
+    key_pair = to_sibling(1, KEY, REST, 5)
     value_rows = along_row(1, VALUE, value_pair)
-    held[1, KEY] = key_terms(HALF, even)
+    hold(1, KEY, REST, 4)
     key_rows = along_row(1, KEY, key_pair)
+    value_first = to_sibling(1, VALUE, FIRST, 3)
+    key_first = to_sibling(1, KEY, FIRST, 3)
+    hold(1, VALUE, FIRST, 2)
+    hold(1, KEY, FIRST, 2)
 
     for half in (0, 1):
         for parity in (0, 1):
             start = half * HALF + parity * QUAD
             kt[start : start + QUAD, :] = kv[half, parity].reshape(QUAD, 2 * D)[:, :D]
     kt[SPAN:, :] = ck_in[...]
-    dckv_out[:, D:] = value_terms(SPAN, ((OWN_CHUNK, ROWS),), 0).astype(BF16)
-    dckv_out[:, :D] = key_terms(SPAN, ((OWN_CHUNK, ROWS),)).astype(BF16)
+    value_first.wait_recv()
     z_value = to_partner(VALUE, value_rows)
+    key_first.wait_recv()
     z_key = to_partner(KEY, key_rows)
 
-    near_value_pair = to_sibling(0, VALUE, value_terms(QUAD, ((1, QUAD),), 0))
-    near_key_pair = to_sibling(0, KEY, key_terms(QUAD, ((1, QUAD),)))
-    held[0, VALUE] = value_terms(0, ((0, QUAD),), 1)
-    held[0, KEY] = key_terms(0, ((0, QUAD),))
+    near_value_pair = to_sibling(0, VALUE, ALL, 1)
+    near_key_pair = to_sibling(0, KEY, ALL, 1)
+    hold(0, VALUE, ALL, 0)
+    hold(0, KEY, ALL, 0)
     near_value_rows = along_row(0, VALUE, near_value_pair)
     near_key_rows = along_row(0, KEY, near_key_pair)
 
+    dckv_out[:, D:] = value_terms(SPAN, ROWS, OWN_CHUNK, 0).astype(BF16)
+    dckv_out[:, :D] = key_terms(SPAN, ROWS, OWN_CHUNK, 0).astype(BF16)
     keys_t = kt[...].T
     for h in range(HEADS):
         dquery = mm(keys_t, dss[:, h * ROWS : (h + 1) * ROWS])
@@ -339,8 +347,8 @@
             dma((4,)),
             dma((2, 2, 4)),
             dma((2, 2, 4)),
-            dma((2, 2)),
-            dma((2, 2)),
+            dma((2, 2, 2)),
+            dma((2, 2, 2)),
             dma((6,)),
             dma((6,)),
         ],

time: 51.7 us -> 51.3 us (level)
  no operation moved by 1% of the time
where the time goes in v3:
time: 51.3 us; the launch traced here: 51.2 us
  Pallas kernels  47.1 us (92%)
  local copies, waits for them, and re-layouts  2.08 us (4%)
  between operations  1.93 us (4%)
    pallas_call x1, Pallas kernels, shards(): pl.pallas_call(kernel, name='attention_backward', out_shape=[vmem((ROWS,...  47.1 us
    slice x2, local copies, waits for them, and re-layouts, shards(): return (dquery, dcomp[:, :D], dcomp[:, D:], dprompt[:, :D], dprompt[:, D:])  1.28 us

profile of v3, /device:TPU:1, one launch (start us, length us, event | category | flops | bytes accessed | tf_op | source)
XLA Modules:
  0.0 51.2 jit_solution(17658193223635632009)
XLA Ops:
  1.9 47.1 %attention_backward.1 = (bf16[256,1024]{1,0:T(8,128)(2,1)S(1)}, bf16[256,256]{1,0:T(8,128)(2,1)S(1)}, bf16[96,256]{1,0:T(8,128)(2,1)S(1)}) custom-call(bf16[256,1024]{1,0:T(8,128)(2,1)} %q_hbm.1, bf16[256,128]{1,0:T(8,128)(2,1)} %ck_hbm.1, bf16[256,128]{1,0:T(8,128)(2,1)} %cv_hbm.1, bf16[96,128]{1,0:T(8,128)(2,1)} %pk_hbm.1, bf16[96,128]{1,0:T(8,128)(2,1)} %pv_hbm.1, ...), custom_call_target="tpu_custom_call" | custom-call | tf_op jit(solution)/shard_map/attention_backward/pallas_call | solution.py:298
  49.1 0.8 %copy.14 = bf16[256,1024]{1,0:T(8,128)(2,1)} copy(bf16[256,1024]{1,0:T(8,128)(2,1)S(1)} %get-tuple-element.15) | data formatting | bytes 1048576
  49.9 0.6 %fusion.1 = (bf16[96,128]{1,0:T(8,128)(2,1)}, bf16[96,128]{1,0:T(8,128)(2,1)}) fusion(bf16[96,256]{1,0:T(8,128)(2,1)S(1)} %get-tuple-element.10), kind=kLoop, calls=%fused_computation.1 | loop fusion | bytes 98304 | tf_op jit(solution)/shard_map/slice | solution.py:359
  50.5 0.7 %fusion = (bf16[256,128]{1,0:T(8,128)(2,1)}, bf16[256,128]{1,0:T(8,128)(2,1)}) fusion(bf16[256,256]{1,0:T(8,128)(2,1)S(1)} %get-tuple-element.9), kind=kLoop, calls=%fused_computation | loop fusion | bytes 262144 | tf_op jit(solution)/shard_map/slice | solution.py:359

commit v4 on v3

--- a/solution.py
+++ b/solution.py
@@ -148,7 +148,6 @@
     scores_of(ck_in[...], cv_in[...], SPAN, OWN_CHUNK, key_pos <= query_pos)
 
     forward(0, along, beside)
-    prompt_scores(0, 0, ALL, 0)
 
     kv_z.wait_recv()
     near_beside = beside
@@ -161,6 +160,7 @@
         )
         for dx in PEERS
     }
+    prompt_scores(0, 0, ALL, 0)
     for copy in near_beside.values():
         copy.wait_recv()
     prompt_scores(0, 1, ALL, 1)

time: 51.3 us -> 50.3 us (0.981)
  Pallas kernels: 47.1 us -> 46.1 us
    pallas_call x1, Pallas kernels: 47.1 us -> 46.1 us  [shards(): pl.pallas_call(kernel, name='attention_backward', out_shape=[vmem((ROWS,...]
where the time goes in v4:
time: 50.3 us; the launch traced here: 50.1 us
  Pallas kernels  46.1 us (92%)
  local copies, waits for them, and re-layouts  2.08 us (4%)
  between operations  1.93 us (4%)
    pallas_call x1, Pallas kernels, shards(): pl.pallas_call(kernel, name='attention_backward', out_shape=[vmem((ROWS,...  46.1 us
    slice x2, local copies, waits for them, and re-layouts, shards(): return (dquery, dcomp[:, :D], dcomp[:, D:], dprompt[:, :D], dprompt[:, D:])  1.28 us

profile of v4, /device:TPU:1, one launch (start us, length us, event | category | flops | bytes accessed | tf_op | source)
XLA Modules:
  0.0 50.1 jit_solution(15962262789764807088)
XLA Ops:
  1.9 46.1 %attention_backward.1 = (bf16[256,1024]{1,0:T(8,128)(2,1)S(1)}, bf16[256,256]{1,0:T(8,128)(2,1)S(1)}, bf16[96,256]{1,0:T(8,128)(2,1)S(1)}) custom-call(bf16[256,1024]{1,0:T(8,128)(2,1)} %q_hbm.1, bf16[256,128]{1,0:T(8,128)(2,1)} %ck_hbm.1, bf16[256,128]{1,0:T(8,128)(2,1)} %cv_hbm.1, bf16[96,128]{1,0:T(8,128)(2,1)} %pk_hbm.1, bf16[96,128]{1,0:T(8,128)(2,1)} %pv_hbm.1, ...), custom_call_target="tpu_custom_call" | custom-call | tf_op jit(solution)/shard_map/attention_backward/pallas_call | solution.py:298
  48.0 0.8 %copy.14 = bf16[256,1024]{1,0:T(8,128)(2,1)} copy(bf16[256,1024]{1,0:T(8,128)(2,1)S(1)} %get-tuple-element.15) | data formatting | bytes 1048576
  48.8 0.6 %fusion.1 = (bf16[96,128]{1,0:T(8,128)(2,1)}, bf16[96,128]{1,0:T(8,128)(2,1)}) fusion(bf16[96,256]{1,0:T(8,128)(2,1)S(1)} %get-tuple-element.10), kind=kLoop, calls=%fused_computation.1 | loop fusion | bytes 98304 | tf_op jit(solution)/shard_map/slice | solution.py:359
  49.5 0.7 %fusion = (bf16[256,128]{1,0:T(8,128)(2,1)}, bf16[256,128]{1,0:T(8,128)(2,1)}) fusion(bf16[256,256]{1,0:T(8,128)(2,1)S(1)} %get-tuple-element.9), kind=kLoop, calls=%fused_computation | loop fusion | bytes 262144 | tf_op jit(solution)/shard_map/slice | solution.py:359
